TPU v7x, 32 devices: a whole 2x2x4 slice. The times are simulated.
32 devices in a mesh: pipe: 4 (over y, core), dp: 4 (over z), tensor: 2 (over x).
Axes of the slice: x: 2, y: 2, z: 4, core: 2. Of those that a mesh axis runs over, the one named last changes fastest.
Arguments:
- grad_out: bfloat16 [4, 4, 4, 96, 6144], P('pipe', None, 'dp'), may hold values from -6 to 6
- qkv_saved: bfloat16 [4, 4, 4, 96, 2, 384], P('pipe', None, 'dp', None, 'tensor'), may hold values from -5 to 5
- w_out: bfloat16 [4, 6144, 2, 128], P('pipe', None, 'tensor'), may hold values from -0.078125 to 0.078125
- w_qkv: bfloat16 [4, 6144, 2, 384], P('pipe', None, 'tensor'), may hold values from -0.21875 to 0.21875
- plan: int32 [4, 4], P('pipe'), may hold values from 0 to 3, each once within a row
Outputs:
- input_grad: bfloat16 [4, 4, 96, 2, 6144], P('pipe', 'dp', 'tensor')
- out_proj_grad: float32 [4, 6144, 2, 128], P('pipe', 'dp', 'tensor')
All inputs are finite; a program needn't handle non-finite values.
Results may differ from a plain program's by a relative error of at most 0.028.
Values may be sent and summed in bfloat16 or wider, within the bound.
A program may use at most 64 MiB of HBM per device.

v0:
```python
import functools

import jax
import jax.numpy as jnp
from jax import lax
from jax.experimental import pallas as pl
from jax.experimental.pallas import tpu as pltpu
from jax.sharding import PartitionSpec as P

BMICRO = 2
PIECES = 8
FAR = [0, 2, 4, 6]
NEAR = [1, 3, 5, 7]
ORDER = [1, 0, 3, 2, 5, 4, 7, 6]
PARTS = 2
MESH = pl.DeviceIdType.MESH


def shifted(block, axis, distance):
    devices = range(lax.axis_size(axis))
    route = [(i - distance, i) for i in devices if i - distance in devices]
    return lax.ppermute(block, axis, route)


def head_forward(queries, key_rows, values):
    score_scale = queries.shape[-1] ** (-0.5)
    scores = jnp.dot(queries, key_rows.T, preferred_element_type=jnp.float32) * score_scale
    row_ids = lax.broadcasted_iota(jnp.int32, scores.shape, 0)
    col_ids = lax.broadcasted_iota(jnp.int32, scores.shape, 1)
    scores = jnp.where(col_ids <= row_ids, scores, -1e30)
    row_max = jnp.max(scores, axis=1, keepdims=True)
    weights = jnp.exp(scores - row_max)
    softmax = weights / jnp.sum(weights, axis=1, keepdims=True)
    soft_low = softmax.astype(jnp.bfloat16)
    attended = jnp.dot(soft_low, values, preferred_element_type=jnp.float32).astype(jnp.bfloat16)
    return (softmax, soft_low, attended)


def head_backward(queries, key_rows, values, softmax, soft_low, attended, grad_head):
    score_scale = queries.shape[-1] ** (-0.5)
    row_dot = jnp.sum(
        grad_head.astype(jnp.float32) * attended.astype(jnp.float32), axis=1, keepdims=True
    )
    grad_values = jnp.dot(soft_low.T, grad_head, preferred_element_type=jnp.float32)
    grad_probs = jnp.dot(grad_head, values.T, preferred_element_type=jnp.float32)
    grad_scores = (softmax * (grad_probs - row_dot)).astype(jnp.bfloat16)
    grad_query = jnp.dot(grad_scores, key_rows, preferred_element_type=jnp.float32) * score_scale
    grad_keys = jnp.dot(grad_scores.T, queries, preferred_element_type=jnp.float32) * score_scale
    return jnp.concatenate([grad_query, grad_keys, grad_values], axis=1).astype(jnp.bfloat16)


def body(grad_out, qkv_saved, w_out, w_qkv, plan):
    gradients = grad_out[0, :, 0]
    saved_qkv = qkv_saved[0, :, 0, :, 0]
    out_proj = w_out[0, :, 0]
    qkv_proj = w_qkv[0, :, 0]
    head_size = out_proj.shape[1]
    seq_len = gradients.shape[1]
    queries = saved_qkv[:, :, :head_size]
    key_rows = saved_qkv[:, :, head_size : 2 * head_size]
    values = saved_qkv[:, :, 2 * head_size :]
    softmax, soft_low, attended = jax.vmap(head_forward)(queries, key_rows, values)
    current = plan[0, :BMICRO]
    grad_current = jnp.take(gradients, current, axis=0)
    grad_heads = jnp.einsum(
        "msd,dh->msh", grad_current, out_proj, preferred_element_type=jnp.float32
    ).astype(jnp.bfloat16)
    grad_qkv = jax.vmap(head_backward)(
        jnp.take(queries, current, axis=0),
        jnp.take(key_rows, current, axis=0),
        jnp.take(values, current, axis=0),
        jnp.take(softmax, current, axis=0),
        jnp.take(soft_low, current, axis=0),
        jnp.take(attended, current, axis=0),
        grad_heads,
    )
    share_rows = seq_len // lax.axis_size("tensor")
    partials = jnp.einsum("bsk,dk->sbd", grad_qkv, qkv_proj, preferred_element_type=jnp.float32)
    summed = lax.psum(partials.astype(jnp.bfloat16), "tensor").astype(jnp.float32)
    own_rows = lax.dynamic_slice_in_dim(
        summed, lax.axis_index("tensor") * share_rows, share_rows, 0
    )
    received = shifted(own_rows.astype(jnp.bfloat16), "pipe", -1)
    weight_grad = lax.psum_scatter(
        jnp.einsum("msc,msh->ch", gradients, attended, preferred_element_type=jnp.float32),
        "dp",
        scatter_dimension=0,
        tiled=True,
    )
    return (received[None, None], weight_grad[None, :, None, :])


def mm(left, right, left_dim, right_dim):
    return lax.dot_general(
        left, right, (((left_dim,), (right_dim,)), ((), ())), preferred_element_type=jnp.float32
    )


def fused_kernel(
    sizes, plan_ref, g_hbm, qkv_hbm, wo_hbm, wq_hbm, in_ref, wg_ref,
    g, qkv, wo, wq, probs, att, gqkv, total, xs, own, xr, fr, hr, fo, ys, rs, rr, ls, lr,
    load_sem, x_send, x_recv, y_send, y_recv, f_send, f_recv, h_send, h_recv, o_send, o_recv, r_send, r_recv, l_send, l_recv,
):
    n, sections, micro, seq, head, features = sizes
    p = lax.axis_index("pipe")
    z = lax.axis_index("dp")
    x = lax.axis_index("tensor")
    scale = head ** (-0.5)
    half = seq // 2
    rows = BMICRO * half
    width = features // PIECES
    chunk = features // n
    part = chunk // PARTS
    items = (n - 1) * PARTS

    loads = [
        pltpu.make_async_copy(src, dst, load_sem.at[i])
        for i, (src, dst) in enumerate(((qkv_hbm, qkv), (g_hbm, g), (wo_hbm, wo), (wq_hbm, wq)))
    ]
    loads[0].start()
    loads[1].start()

    barrier = pltpu.get_barrier_semaphore()

    def greet(target):
        pl.semaphore_signal(barrier, inc=1, device_id=target, device_id_type=MESH)

    @pl.when(z > 0)
    def _():
        greet({"dp": z - 1})

    @pl.when(z < n - 1)
    def _():
        greet({"dp": z + 1})

    @pl.when(p > 0)
    def _():
        greet({"tensor": 1 - x})

    @pl.when(p < sections - 1)
    def _():
        greet({"pipe": p + 1})

    def x_copy(k):
        return pltpu.make_async_remote_copy(
            src_ref=xs.at[k], dst_ref=xr.at[k], send_sem=x_send.at[k], recv_sem=x_recv.at[k],
            device_id={"tensor": 1 - x}, device_id_type=MESH,
        )

    def y_copy(k):
        return pltpu.make_async_remote_copy(
            src_ref=ys.at[k], dst_ref=in_ref.at[:, :, pl.ds(k * width, width)],
            send_sem=y_send.at[k], recv_sem=y_recv.at[k],
            device_id={"pipe": p - 1}, device_id_type=MESH,
        )

    def f_copy(k):
        return pltpu.make_async_remote_copy(
            src_ref=xs.at[k], dst_ref=fr.at[k // 2], send_sem=f_send.at[k // 2], recv_sem=f_recv.at[k // 2],
            device_id={"pipe": p - 1}, device_id_type=MESH,
        )

    def h_copy(k):
        return pltpu.make_async_remote_copy(
            src_ref=own.at[k], dst_ref=hr.at[k // 2], send_sem=h_send.at[k // 2], recv_sem=h_recv.at[k // 2],
            device_id={"pipe": p - 1}, device_id_type=MESH,
        )

    def o_copy(k):
        return pltpu.make_async_remote_copy(
            src_ref=fr.at[k // 2], dst_ref=fo.at[k // 2], send_sem=o_send.at[k // 2], recv_sem=o_recv.at[k // 2],
            device_id={"tensor": 1 - x}, device_id_type=MESH,
        )

    def r_copy(i):
        return pltpu.make_async_remote_copy(
            src_ref=rs.at[i], dst_ref=rr.at[i], send_sem=r_send.at[i], recv_sem=r_recv.at[i],
            device_id={"dp": z + 1}, device_id_type=MESH,
        )

    def l_copy(i):
        return pltpu.make_async_remote_copy(
            src_ref=ls.at[i], dst_ref=lr.at[i], send_sem=l_send.at[i], recv_sem=l_recv.at[i],
            device_id={"dp": z - 1}, device_id_type=MESH,
        )

    def r_columns(i):
        return pl.ds((n - 1 - i // PARTS) * chunk + (i % PARTS) * part, part)

    def l_columns(i):
        return pl.ds((i // PARTS) * chunk + (i % PARTS) * part, part)

    loads[0].wait()
    keep = lax.broadcasted_iota(jnp.int32, (seq, seq), 1) <= lax.broadcasted_iota(jnp.int32, (seq, seq), 0)
    softs = []
    for m in range(micro):
        scores = mm(qkv[m, :, :head], qkv[m, :, head : 2 * head], 1, 1) * scale
        scores = jnp.where(keep, scores, -1e30)
        weights = jnp.exp(scores - jnp.max(scores, axis=1, keepdims=True))
        softs.append(weights / jnp.sum(weights, axis=1, keepdims=True))
    outs = [
        mm(softs[m].astype(jnp.bfloat16), qkv[m, :, 2 * head :], 1, 0).astype(jnp.bfloat16)
        for m in range(micro)
    ]
    for m in range(micro):
        probs[m] = softs[m]
        att[m] = outs[m]
    loads[2].start()
    loads[3].start()

    peers = lax.div(z + n - 1, n) + lax.div(2 * n - 2 - z, n) + 2 * lax.div(p + sections - 1, sections)
    pl.semaphore_wait(barrier, peers)

    loads[1].wait()

    upper = lax.div(z, n // 2)

    def product(i):
        place = upper * (i // PARTS) + (1 - upper) * (n - 1 - i // PARTS)
        columns = pl.ds(pl.multiple_of(place * chunk + (i % PARTS) * part, part), part)
        value = mm(
            att[...].reshape(micro * seq, head), g[:, :, columns].reshape(micro * seq, part), 0, 0
        )
        total[:, columns] = value
        if i < items:

            @pl.when(z == 0)
            def _():
                rs[i] = value.astype(jnp.bfloat16)
                r_copy(i).start()

            @pl.when(z == n - 1)
            def _():
                ls[i] = value.astype(jnp.bfloat16)
                l_copy(i).start()

    for i in range(PARTS):
        product(i)

    loads[2].wait()
    loads[3].wait()

    @pl.when(p > 0)
    def _():
        chosen = [plan_ref[0, j] for j in range(BMICRO)]
        acc = jnp.zeros((BMICRO * seq, head), jnp.float32)
        for k in range(PIECES):
            columns = pl.ds(k * width, width)
            lhs = jnp.concatenate([g[m, :, columns] for m in chosen], axis=0)
            acc = acc + mm(lhs, wo[columns, :], 1, 0)
        heads = []
        for j in range(BMICRO):
            m = chosen[j]
            grad_head = acc[j * seq : (j + 1) * seq].astype(jnp.bfloat16)
            softmax = probs[m]
            soft_low = softmax.astype(jnp.bfloat16)
            row_dot = jnp.sum(
                grad_head.astype(jnp.float32) * att[m].astype(jnp.float32), axis=1, keepdims=True
            )
            grad_values = mm(soft_low, grad_head, 0, 0)
            grad_probs = mm(grad_head, qkv[m, :, 2 * head :], 1, 1)
            grad_scores = (softmax * (grad_probs - row_dot)).astype(jnp.bfloat16)
            grad_query = mm(grad_scores, qkv[m, :, head : 2 * head], 1, 0) * scale
            grad_keys = mm(grad_scores, qkv[m, :, :head], 0, 0) * scale
            heads.append(jnp.concatenate([grad_query, grad_keys, grad_values], axis=1).astype(jnp.bfloat16))
        row = lax.broadcasted_iota(jnp.int32, (2 * rows, 2 * rows), 0)
        column = lax.broadcasted_iota(jnp.int32, (2 * rows, 2 * rows), 1)
        second = (row >= rows).astype(jnp.int32)
        side = second * x + (1 - second) * (1 - x)
        inner = row - second * rows
        token = lax.shift_right_logical(inner, 1)
        source = (inner - 2 * token) * seq + side * half + token
        order = (column == source).astype(jnp.bfloat16)
        gqkv[...] = mm(order, jnp.concatenate(heads, axis=0), 1, 0).astype(jnp.bfloat16)
        for k in ORDER:
            term = mm(gqkv[...], wq[pl.ds(k * width, width), :], 1, 1).astype(jnp.bfloat16)
            xs[k] = term[:rows]
            own[k] = term[rows:]
            if k in FAR:

                @pl.when(p == 2)
                def _():
                    f_copy(k).start()

                @pl.when(p != 2)
                def _():
                    x_copy(k).start()

            else:
                x_copy(k).start()

        @pl.when(p == 2)
        def _():
            for k in FAR:
                h_copy(k).start()

    for i in range(PARTS, items + PARTS):
        product(i)

    @pl.when(p == sections - 1)
    def _():
        in_ref[...] = jnp.zeros_like(in_ref)

    def summed(mine, other):
        value = mine.astype(jnp.float32) + other.astype(jnp.float32)
        return value.reshape(half, BMICRO, width).astype(jnp.bfloat16)

    def do_x(k):
        x_copy(k).wait_recv()
        ys[k] = summed(own[k], xr[k])
        y_copy(k).start()

    def do_odd(k):
        @pl.when((p == 1) | (p == 3))
        def _():
            do_x(k)

    def do_two(k):
        @pl.when(p == 2)
        def _():
            do_x(k)

    def pass_on(k):
        @pl.when(p == 1)
        def _():
            f_copy(k).wait_recv()
            o_copy(k).start()

    def finish(k):
        @pl.when(p == 1)
        def _():
            h_copy(k).wait_recv()
            o_copy(k).wait_recv()
            in_ref[:, :, pl.ds(k * width, width)] = summed(hr[k // 2], fo[k // 2])

    def do_z(i):
        right_chunk = n - 1 - i // PARTS
        left_chunk = i // PARTS
        right_cols, left_cols = r_columns(i), l_columns(i)

        @pl.when((z > 0) & (z < right_chunk))
        def _():
            r_copy(i).wait_recv()
            rs[i] = (total[:, right_cols] + rr[i].astype(jnp.float32)).astype(jnp.bfloat16)
            r_copy(i).start()

        @pl.when((z < n - 1) & (z > left_chunk))
        def _():
            l_copy(i).wait_recv()
            ls[i] = (total[:, left_cols] + lr[i].astype(jnp.float32)).astype(jnp.bfloat16)
            l_copy(i).start()

        @pl.when(z == right_chunk)
        def _():
            r_copy(i).wait_recv()
            total[:, right_cols] = total[:, right_cols] + rr[i].astype(jnp.float32)

        @pl.when(z == left_chunk)
        def _():
            l_copy(i).wait_recv()
            total[:, left_cols] = total[:, left_cols] + lr[i].astype(jnp.float32)

    events = [(5.0 + 26.0 * (i + 1) / items, do_z, i) for i in range(items)]
    events += [(8.5 + 2.4 * (i + 1), do_odd, k) for i, k in enumerate(ORDER)]
    events += [(8.5 + 3.6 * (i + 1), do_two, k) for i, k in enumerate(NEAR)]
    events += [(10.5 + 3.6 * i, pass_on, k) for i, k in enumerate(FAR)]
    events += [(29.0 + i, finish, k) for i, k in enumerate(FAR)]
    for _, act, index in sorted(events, key=lambda e: e[0]):
        act(index)

    for i in range(PARTS):
        columns = pl.ds(pl.multiple_of(z * chunk + i * part, part), part)
        wg_ref[i * part : (i + 1) * part, :] = total[:, columns].T

    @pl.when(p < sections - 1)
    def _():
        for k in NEAR:
            y_copy(k).wait_recv()

    @pl.when((p == 0) | (p == 2))
    def _():
        for k in FAR:
            y_copy(k).wait_recv()

    @pl.when(p > 0)
    def _():
        for k in NEAR:
            x_copy(k).wait_send()
            y_copy(k).wait_send()

    @pl.when((p == 1) | (p == 3))
    def _():
        for k in FAR:
            x_copy(k).wait_send()
            y_copy(k).wait_send()

    @pl.when(p == 2)
    def _():
        for k in FAR:
            f_copy(k).wait_send()
            h_copy(k).wait_send()

    @pl.when(p == 1)
    def _():
        for k in FAR:
            o_copy(k).wait_send()

    for i in range(items):

        @pl.when(z < n - 1 - i // PARTS)
        def _():
            r_copy(i).wait_send()

        @pl.when(z > i // PARTS)
        def _():
            l_copy(i).wait_send()


def copy_kernel(in_from, wg_from, in_to, wg_to, sem):
    tokens, rows = in_from.shape[0] // 4, wg_from.shape[0] // 4
    copies = []
    for i in range(4):
        cut = pl.ds(i * tokens, tokens)
        copies.append(pltpu.make_async_copy(in_from.at[cut], in_to.at[cut], sem.at[i]))
        cut = pl.ds(i * rows, rows)
        copies.append(pltpu.make_async_copy(wg_from.at[cut], wg_to.at[cut], sem.at[4 + i]))
    for copy in copies:
        copy.start()
    for copy in copies:
        copy.wait()


def fused_body(n, sections, grad_out, qkv_saved, w_out, w_qkv, plan):
    _, micro, _, seq, features = grad_out.shape
    head = w_out.shape[-1]
    half = seq // 2
    rows = BMICRO * half
    width = features // PIECES
    part = features // n // PARTS
    items = (n - 1) * PARTS
    low, full = jnp.bfloat16, jnp.float32
    dma = pltpu.SemaphoreType.DMA
    strip = (items, head, part)
    term = (PIECES, rows, width)
    anywhere = pl.BlockSpec(memory_space=pl.ANY)
    vmem = pl.BlockSpec(memory_space=pltpu.VMEM)
    received, weight_grad = pl.pallas_call(
        functools.partial(fused_kernel, (n, sections, micro, seq, head, features)),
        out_shape=(
            jax.ShapeDtypeStruct((half, BMICRO, features), low),
            jax.ShapeDtypeStruct((features // n, head), full),
        ),
        in_specs=[pl.BlockSpec(memory_space=pltpu.SMEM)] + [anywhere] * 4,
        out_specs=(vmem, vmem),
        scratch_shapes=[
            pltpu.VMEM((micro, seq, features), low),
            pltpu.VMEM((micro, seq, 3 * head), low),
            pltpu.VMEM((features, head), low),
            pltpu.VMEM((features, 3 * head), low),
            pltpu.VMEM((micro, seq, seq), full),
            pltpu.VMEM((micro, seq, head), low),
            pltpu.VMEM((2 * rows, 3 * head), low),
            pltpu.VMEM((head, features), full),
        ]
        + [pltpu.VMEM(term, low)] * 3
        + [pltpu.VMEM((len(FAR), rows, width), low)] * 3
        + [pltpu.VMEM((PIECES, half, BMICRO, width), low)]
        + [pltpu.VMEM(strip, low)] * 4
        + [dma((4,))]
        + [dma((PIECES,))] * 4
        + [dma((len(FAR),))] * 6
        + [dma((items,))] * 4,
        compiler_params=pltpu.CompilerParams(
            collective_id=0, has_side_effects=True, vmem_limit_bytes=56 * 1024 * 1024
        ),
        cost_estimate=pl.CostEstimate(flops=2_000_000_000, bytes_accessed=14_000_000, transcendentals=40_000),
    )(
        plan,
        grad_out.reshape(micro, seq, features),
        qkv_saved.reshape(micro, seq, 3 * head),
        w_out.reshape(features, head),
        w_qkv.reshape(features, 3 * head),
    )
    received, weight_grad = pl.pallas_call(
        copy_kernel,
        out_shape=(
            jax.ShapeDtypeStruct(received.shape, low),
            jax.ShapeDtypeStruct(weight_grad.shape, full),
        ),
        in_specs=[anywhere] * 2,
        out_specs=(anywhere, anywhere),
        scratch_shapes=[dma((8,))],
        compiler_params=pltpu.CompilerParams(vmem_limit_bytes=63 * 1024 * 1024),
    )(received, weight_grad)
    return (received[None, None], weight_grad[None, :, None, :])


def solution(mesh):
    in_specs = (
        P("pipe", None, "dp", None, None),
        P("pipe", None, "dp", None, "tensor", None),
        P("pipe", None, "tensor", None),
        P("pipe", None, "tensor", None),
        P("pipe", None),
    )
    out_specs = (P("pipe", "dp", "tensor", None, None), P("pipe", "dp", "tensor", None))
    chosen = body
    if (mesh.shape["pipe"], mesh.shape["dp"], mesh.shape["tensor"]) == (4, 4, 2):
        chosen = functools.partial(fused_body, mesh.shape["dp"], mesh.shape["pipe"])
    return jax.shard_map(chosen, mesh=mesh, in_specs=in_specs, out_specs=out_specs, check_vma=False)
```

profile of v0, /device:TPU:1, one launch (start us, length us, event | category | flops | bytes accessed | tf_op | source)
XLA Modules:
  0.0 112.3 jit_solution(6970786130462317967)
XLA Ops:
  0.6 51.0 %shard_map.68 = (bf16[48,2,6144]{2,1,0:T(2,128)(2,1)}, f32[1536,128]{1,0:T(8,128)}) custom-call(s32[1,4]{1,0:T(1,128)} %plan_ref.1, bf16[4,96,6144]{2,1,0:T(8,128)(2,1)} %bitcast.8, bf16[4,96,384]{2,1,0:T(8,128)(2,1)} %bitcast.11, bf16[6144,128]{1,0:T(8,128)(2,1)} %bitcast.10, bf16[6144,384]{1,0:T(8,128)(2,1)} %bitcast.9), custom_call_target="tpu_custom_call" | custom-call | flops 2000000000 | bytes 14000000 | tf_op jit(solution)/shard_map/pallas_call | solution.py:447
  51.6 60.7 %shard_map.69 = (bf16[48,2,6144]{2,1,0:T(2,128)(2,1)}, f32[1536,128]{1,0:T(8,128)}) custom-call(bf16[48,2,6144]{2,1,0:T(2,128)(2,1)} %get-tuple-element.6.in_from, f32[1536,128]{1,0:T(8,128)} %get-tuple-element.7.wg_from), custom_call_target="tpu_custom_call" | custom-call | tf_op jit(solution)/shard_map/pallas_call | solution.py:484
where the time goes:
time: 114 us; the launch traced here: 112 us
  Pallas kernels  112 us (98%)
    pallas_call x1, Pallas kernels, fused_body(): pl.pallas_call(copy_kernel, out_shape=(jax.ShapeDtypeStruct(received.shap...  60.7 us
    pallas_call x1, Pallas kernels, fused_body(): pl.pallas_call(functools.partial(fused_kernel, (n, sections, micro, seq,...  51 us

commit v1 on v0

--- a/solution.py
+++ b/solution.py
@@ -98,7 +98,7 @@
 
 def fused_kernel(
     sizes, plan_ref, g_hbm, qkv_hbm, wo_hbm, wq_hbm, in_ref, wg_ref,
-    g, qkv, wo, wq, probs, att, gqkv, total, xs, own, xr, fr, hr, fo, ys, rs, rr, ls, lr,
+    g, qkv, wo, wq, probs, att, att_t, gqkv, total, xs, own, xr, fr, hr, fo, ys, rs, rr, ls, lr,
     load_sem, x_send, x_recv, y_send, y_recv, f_send, f_recv, h_send, h_recv, o_send, o_recv, r_send, r_recv, l_send, l_recv,
 ):
     n, sections, micro, seq, head, features = sizes
@@ -205,6 +205,7 @@
     for m in range(micro):
         probs[m] = softs[m]
         att[m] = outs[m]
+    att_t[...] = jnp.concatenate(outs, axis=0).T
     loads[2].start()
     loads[3].start()
 
@@ -219,7 +220,7 @@
         place = upper * (i // PARTS) + (1 - upper) * (n - 1 - i // PARTS)
         columns = pl.ds(pl.multiple_of(place * chunk + (i % PARTS) * part, part), part)
         value = mm(
-            att[...].reshape(micro * seq, head), g[:, :, columns].reshape(micro * seq, part), 0, 0
+            att_t[...], g[:, :, columns].reshape(micro * seq, part), 1, 0
         )
         total[:, columns] = value
         if i < items:
@@ -237,11 +238,14 @@
     for i in range(PARTS):
         product(i)
 
-    loads[2].wait()
-    loads[3].wait()
+    @pl.when(p == 0)
+    def _():
+        loads[2].wait()
+        loads[3].wait()
 
     @pl.when(p > 0)
     def _():
+        loads[2].wait()
         chosen = [plan_ref[0, j] for j in range(BMICRO)]
         acc = jnp.zeros((BMICRO * seq, head), jnp.float32)
         for k in range(PIECES):
@@ -272,6 +276,7 @@
         source = (inner - 2 * token) * seq + side * half + token
         order = (column == source).astype(jnp.bfloat16)
         gqkv[...] = mm(order, jnp.concatenate(heads, axis=0), 1, 0).astype(jnp.bfloat16)
+        loads[3].wait()
         for k in ORDER:
             term = mm(gqkv[...], wq[pl.ds(k * width, width), :], 1, 1).astype(jnp.bfloat16)
             xs[k] = term[:rows]
@@ -333,38 +338,44 @@
             o_copy(k).wait_recv()
             in_ref[:, :, pl.ds(k * width, width)] = summed(hr[k // 2], fo[k // 2])
 
-    def do_z(i):
-        right_chunk = n - 1 - i // PARTS
-        left_chunk = i // PARTS
-        right_cols, left_cols = r_columns(i), l_columns(i)
-
-        @pl.when((z > 0) & (z < right_chunk))
+    def add_right(i, hop):
+        place = n - 1 - i // PARTS
+        columns = r_columns(i)
+
+        @pl.when(z == hop + 1)
         def _():
             r_copy(i).wait_recv()
-            rs[i] = (total[:, right_cols] + rr[i].astype(jnp.float32)).astype(jnp.bfloat16)
-            r_copy(i).start()
-
-        @pl.when((z < n - 1) & (z > left_chunk))
+            value = total[:, columns] + rr[i].astype(jnp.float32)
+            if hop + 1 < place:
+                rs[i] = value.astype(jnp.bfloat16)
+                r_copy(i).start()
+            else:
+                total[:, columns] = value
+
+    def add_left(i, hop):
+        place = i // PARTS
+        columns = l_columns(i)
+
+        @pl.when(z == n - 2 - hop)
         def _():
             l_copy(i).wait_recv()
-            ls[i] = (total[:, left_cols] + lr[i].astype(jnp.float32)).astype(jnp.bfloat16)
-            l_copy(i).start()
-
-        @pl.when(z == right_chunk)
-        def _():
-            r_copy(i).wait_recv()
-            total[:, right_cols] = total[:, right_cols] + rr[i].astype(jnp.float32)
-
-        @pl.when(z == left_chunk)
-        def _():
-            l_copy(i).wait_recv()
-            total[:, left_cols] = total[:, left_cols] + lr[i].astype(jnp.float32)
-
-    events = [(5.0 + 26.0 * (i + 1) / items, do_z, i) for i in range(items)]
-    events += [(8.5 + 2.4 * (i + 1), do_odd, k) for i, k in enumerate(ORDER)]
-    events += [(8.5 + 3.6 * (i + 1), do_two, k) for i, k in enumerate(NEAR)]
-    events += [(10.5 + 3.6 * i, pass_on, k) for i, k in enumerate(FAR)]
-    events += [(29.0 + i, finish, k) for i, k in enumerate(FAR)]
+            value = total[:, columns] + lr[i].astype(jnp.float32)
+            if n - 2 - hop > place:
+                ls[i] = value.astype(jnp.bfloat16)
+                l_copy(i).start()
+            else:
+                total[:, columns] = value
+
+    events = []
+    for i in range(items):
+        for hop in range(n - 1 - i // PARTS):
+            due = 6.0 + 4.6 * (i + 1) + 3.5 * hop
+            events.append((due, functools.partial(add_right, hop=hop), i))
+            events.append((due, functools.partial(add_left, hop=hop), i))
+    events += [(11.0 + 2.6 * (i + 1), do_odd, k) for i, k in enumerate(ORDER)]
+    events += [(11.0 + 3.4 * (i + 1), do_two, k) for i, k in enumerate(NEAR)]
+    events += [(10.0 + 3.4 * (i + 1), pass_on, k) for i, k in enumerate(FAR)]
+    events += [(30.0 + i, finish, k) for i, k in enumerate(FAR)]
     for _, act, index in sorted(events, key=lambda e: e[0]):
         act(index)
 
@@ -416,17 +427,21 @@
             l_copy(i).wait_send()
 
 
-def copy_kernel(in_from, wg_from, in_to, wg_to, sem):
+def copy_kernel(in_from, wg_from, in_to, wg_to, in_mid, wg_mid, first, last):
     tokens, rows = in_from.shape[0] // 4, wg_from.shape[0] // 4
-    copies = []
+    arrive, leave = [], []
     for i in range(4):
-        cut = pl.ds(i * tokens, tokens)
-        copies.append(pltpu.make_async_copy(in_from.at[cut], in_to.at[cut], sem.at[i]))
-        cut = pl.ds(i * rows, rows)
-        copies.append(pltpu.make_async_copy(wg_from.at[cut], wg_to.at[cut], sem.at[4 + i]))
-    for copy in copies:
+        pairs = ((in_from, in_mid, in_to, tokens, i), (wg_from, wg_mid, wg_to, rows, 4 + i))
+        for source, middle, target, size, slot in pairs:
+            cut = pl.ds(i * size, size)
+            arrive.append(pltpu.make_async_copy(source.at[cut], middle.at[cut], first.at[slot]))
+            leave.append(pltpu.make_async_copy(middle.at[cut], target.at[cut], last.at[slot]))
+    for copy in arrive:
         copy.start()
-    for copy in copies:
+    for before, after in zip(arrive, leave):
+        before.wait()
+        after.start()
+    for copy in leave:
         copy.wait()
 
 
@@ -459,6 +474,7 @@
             pltpu.VMEM((features, 3 * head), low),
             pltpu.VMEM((micro, seq, seq), full),
             pltpu.VMEM((micro, seq, head), low),
+            pltpu.VMEM((head, micro * seq), low),
             pltpu.VMEM((2 * rows, 3 * head), low),
             pltpu.VMEM((head, features), full),
         ]
@@ -489,7 +505,12 @@
         ),
         in_specs=[anywhere] * 2,
         out_specs=(anywhere, anywhere),
-        scratch_shapes=[dma((8,))],
+        scratch_shapes=[
+            pltpu.VMEM(received.shape, low),
+            pltpu.VMEM(weight_grad.shape, full),
+            dma((8,)),
+            dma((8,)),
+        ],
         compiler_params=pltpu.CompilerParams(vmem_limit_bytes=63 * 1024 * 1024),
     )(received, weight_grad)
     return (received[None, None], weight_grad[None, :, None, :])

time: 114 us -> 39.2 us (0.34)
  the two profiles are of different devices: /device:TPU:1 before, /device:TPU:10 now
where the time goes in v1:
time: 39.2 us; the launch traced here: 39.1 us
  Pallas kernels  38.4 us (98%)
  between operations  0.64 us (2%)
    pallas_call x1, Pallas kernels, fused_body(): pl.pallas_call(functools.partial(fused_kernel, (n, sections, micro, seq,...  36.1 us
    pallas_call x1, Pallas kernels, fused_body(): pl.pallas_call(copy_kernel, out_shape=(jax.ShapeDtypeStruct(received.shap...  2.38 us

profile of v1, /device:TPU:10, one launch (start us, length us, event | category | flops | bytes accessed | tf_op | source)
XLA Modules:
  0.0 39.1 jit_solution(457508086691270529)
XLA Ops:
  0.6 36.1 %shard_map.68 = (bf16[48,2,6144]{2,1,0:T(2,128)(2,1)}, f32[1536,128]{1,0:T(8,128)}) custom-call(s32[1,4]{1,0:T(1,128)} %plan_ref.1, bf16[4,96,6144]{2,1,0:T(8,128)(2,1)} %bitcast.8, bf16[4,96,384]{2,1,0:T(8,128)(2,1)} %bitcast.11, bf16[6144,128]{1,0:T(8,128)(2,1)} %bitcast.10, bf16[6144,384]{1,0:T(8,128)(2,1)} %bitcast.9), custom_call_target="tpu_custom_call" | custom-call | flops 2000000000 | bytes 14000000 | tf_op jit(solution)/shard_map/pallas_call | solution.py:462
  36.7 2.4 %shard_map.69 = (bf16[48,2,6144]{2,1,0:T(2,128)(2,1)}, f32[1536,128]{1,0:T(8,128)}) custom-call(bf16[48,2,6144]{2,1,0:T(2,128)(2,1)} %get-tuple-element.6.in_from, f32[1536,128]{1,0:T(8,128)} %get-tuple-element.7.wg_from), custom_call_target="tpu_custom_call" | custom-call | tf_op jit(solution)/shard_map/pallas_call | solution.py:500

commit v2 on v1

--- a/solution.py
+++ b/solution.py
@@ -12,7 +12,7 @@
 FAR = [0, 2, 4, 6]
 NEAR = [1, 3, 5, 7]
 ORDER = [1, 0, 3, 2, 5, 4, 7, 6]
-PARTS = 2
+PARTS = 4
 MESH = pl.DeviceIdType.MESH
 
 
@@ -235,7 +235,7 @@
                 ls[i] = value.astype(jnp.bfloat16)
                 l_copy(i).start()
 
-    for i in range(PARTS):
+    for i in range(PARTS + 2):
         product(i)
 
     @pl.when(p == 0)
@@ -299,7 +299,7 @@
             for k in FAR:
                 h_copy(k).start()
 
-    for i in range(PARTS, items + PARTS):
+    for i in range(PARTS + 2, items + PARTS):
         product(i)
 
     @pl.when(p == sections - 1)
@@ -349,6 +349,8 @@
             if hop + 1 < place:
                 rs[i] = value.astype(jnp.bfloat16)
                 r_copy(i).start()
+            elif place == n - 1 or place < n // 2:
+                wg_ref[pl.ds((i % PARTS) * part, part), :] = value.T
             else:
                 total[:, columns] = value
 
@@ -363,13 +365,15 @@
             if n - 2 - hop > place:
                 ls[i] = value.astype(jnp.bfloat16)
                 l_copy(i).start()
+            elif place == 0 or place >= n // 2:
+                wg_ref[pl.ds((i % PARTS) * part, part), :] = value.T
             else:
                 total[:, columns] = value
 
     events = []
     for i in range(items):
         for hop in range(n - 1 - i // PARTS):
-            due = 6.0 + 4.6 * (i + 1) + 3.5 * hop
+            due = 6.0 + 26.0 * (i + 1) / items + 2.5 * hop
             events.append((due, functools.partial(add_right, hop=hop), i))
             events.append((due, functools.partial(add_left, hop=hop), i))
     events += [(11.0 + 2.6 * (i + 1), do_odd, k) for i, k in enumerate(ORDER)]
@@ -378,10 +382,6 @@
     events += [(30.0 + i, finish, k) for i, k in enumerate(FAR)]
     for _, act, index in sorted(events, key=lambda e: e[0]):
         act(index)
-
-    for i in range(PARTS):
-        columns = pl.ds(pl.multiple_of(z * chunk + i * part, part), part)
-        wg_ref[i * part : (i + 1) * part, :] = total[:, columns].T
 
     @pl.when(p < sections - 1)
     def _():

time: 39.2 us -> 40.1 us (1.023)
  the two profiles are of different devices: /device:TPU:10 before, /device:TPU:1 now
where the time goes in v2:
time: 40.1 us; the launch traced here: 39.9 us
  Pallas kernels  39.3 us (98%)
  between operations  0.64 us (2%)
    pallas_call x1, Pallas kernels, fused_body(): pl.pallas_call(functools.partial(fused_kernel, (n, sections, micro, seq,...  36.9 us
    pallas_call x1, Pallas kernels, fused_body(): pl.pallas_call(copy_kernel, out_shape=(jax.ShapeDtypeStruct(received.shap...  2.38 us

profile of v2, /device:TPU:1, one launch (start us, length us, event | category | flops | bytes accessed | tf_op | source)
XLA Modules:
  0.0 39.9 jit_solution(4097103859447883603)
XLA Ops:
  0.6 36.9 %shard_map.68 = (bf16[48,2,6144]{2,1,0:T(2,128)(2,1)}, f32[1536,128]{1,0:T(8,128)}) custom-call(s32[1,4]{1,0:T(1,128)} %plan_ref.1, bf16[4,96,6144]{2,1,0:T(8,128)(2,1)} %bitcast.8, bf16[4,96,384]{2,1,0:T(8,128)(2,1)} %bitcast.11, bf16[6144,128]{1,0:T(8,128)(2,1)} %bitcast.10, bf16[6144,384]{1,0:T(8,128)(2,1)} %bitcast.9), custom_call_target="tpu_custom_call" | custom-call | flops 2000000000 | bytes 14000000 | tf_op jit(solution)/shard_map/pallas_call | solution.py:462
  37.5 2.4 %shard_map.69 = (bf16[48,2,6144]{2,1,0:T(2,128)(2,1)}, f32[1536,128]{1,0:T(8,128)}) custom-call(bf16[48,2,6144]{2,1,0:T(2,128)(2,1)} %get-tuple-element.6.in_from, f32[1536,128]{1,0:T(8,128)} %get-tuple-element.7.wg_from), custom_call_target="tpu_custom_call" | custom-call | tf_op jit(solution)/shard_map/pallas_call | solution.py:500
